TPU v7x, 128 devices: a whole 4x4x4 slice. The times are simulated.
128 devices in a mesh: row: 8 (over z, core), col: 16 (over y, x).
Axes of the slice: x: 4, y: 4, z: 4, core: 2. Of those that a mesh axis runs over, the one named last changes fastest.
Arguments:
- p_tiles: float32 [64, 8, 2, 16, 128, 128], P(None, 'row', None, 'col'), may hold values from -0.005859375 to 0.005859375
- active: int32 [128, 8], replicated, may hold values from 0 to 511, as said below
- counts: int32 [128], P(('row', 'col')), may hold values from 1024 to 4096
- basis: bfloat16 [128, 4096, 1024], P(('row', 'col')), may hold values from -6 to 6
- kernel: float32 [128, 4096], P(('row', 'col')), may hold values from -0.09375 to 0.09375
Outputs:
- h_tiles: float32 [64, 8, 2, 16, 128, 128], P(None, 'row', None, 'col')
- density: float32 [128, 4096], P(('row', 'col'))
Inputs may be any that keep to these rules, and one draw needn't show every extreme that they name: `active`: entry t of a batch's list is (s + t + 8 u_t) mod 512 for the batch's start s and u_t of 0 or 1. The tiles that the batches of one device need from one device holding them number at most 1, and every device needs exactly 1 from some holder.
All inputs are finite; a program needn't handle non-finite values.
Results may differ from a plain program's by a relative error of at most 0.0041.
Values may be sent and summed in bfloat16 or wider, within the bound.
A program may use at most 128 MiB of HBM per device.

v0:
```python
import jax
import jax.numpy as jnp
from jax import lax
from jax.sharding import PartitionSpec as P


def batch_whole(values, matrix, kernel_row, point_count):
    total_points = values.shape[0]
    product = jnp.dot(values, matrix, preferred_element_type=jnp.float32)
    inside = jnp.arange(total_points, dtype=jnp.int32) < point_count
    density = jnp.where(
        inside, jnp.sum(product * values.astype(jnp.float32), axis=1), jnp.float32(0.0)
    )
    weighted = ((kernel_row * density)[:, None] * values.astype(jnp.float32)).astype(jnp.bfloat16)
    hamilton = lax.dot_general(
        values, weighted, (((0,), (0,)), ((), ())), preferred_element_type=jnp.float32
    )
    return (hamilton, density)


def local(p_tiles, active, counts, basis, kernel):
    row_count = lax.axis_size("row")
    col_count = lax.axis_size("col")
    device_count = row_count * col_count
    myself = lax.axis_index("row") * col_count + lax.axis_index("col")
    slab_rows, _, offset_groups, _, tile_size, _ = p_tiles.shape
    block_total = slab_rows * row_count
    active_count = active.shape[1]
    batch_count = basis.shape[0]
    span_width = active_count * tile_size
    capacity = batch_count * active_count // row_count
    entries = batch_count * active_count * active_count
    first_block = active[:, :, None] * jnp.ones((1, 1, active_count), jnp.int32)
    second_block = active[:, None, :] * jnp.ones((1, active_count, 1), jnp.int32)
    offset = (second_block - first_block + 2 * active_count) % block_total
    holder = (first_block % row_count * col_count + offset % col_count).reshape(
        device_count, entries
    )
    local_place = (first_block // row_count * offset_groups + offset // col_count).reshape(
        device_count, entries
    )
    is_mine = (holder == myself).astype(jnp.int32)
    slot_rank = jnp.cumsum(is_mine, axis=1) - 1
    slot_index = jnp.arange(capacity, dtype=jnp.int32)
    chosen = (is_mine[:, None, :] == 1) & (slot_rank[:, None, :] == slot_index[None, :, None])
    filled = jnp.any(chosen, axis=2).reshape(device_count * capacity)
    source = jnp.sum(jnp.where(chosen, local_place[:, None, :], 0), axis=2).reshape(
        device_count * capacity
    )
    own_holder = lax.dynamic_index_in_dim(holder, myself, 0, keepdims=False)
    entry_index = jnp.arange(entries, dtype=jnp.int32)
    earlier = (own_holder[:, None] == own_holder[None, :]) & (
        entry_index[None, :] < entry_index[:, None]
    )
    own_rank = jnp.sum(earlier.astype(jnp.int32), axis=1)
    position = own_holder * capacity + own_rank
    flat_tiles = p_tiles.reshape(slab_rows * offset_groups, tile_size, tile_size)
    outgoing = jnp.where(filled[:, None, None], flat_tiles[source], jnp.float32(0.0)).astype(
        jnp.bfloat16
    )
    incoming = lax.all_to_all(outgoing, ("row", "col"), split_axis=0, concat_axis=0, tiled=True)
    gathered = incoming[position].reshape(
        batch_count, active_count, active_count, tile_size, tile_size
    )
    matrices = gathered.transpose(0, 1, 3, 2, 4).reshape(batch_count, span_width, span_width)
    hamilton, density = batch_whole(basis[0], matrices[0], kernel[0], counts[0])
    pieces = hamilton.reshape(active_count, tile_size, active_count, tile_size).transpose(
        0, 2, 1, 3
    )
    pieces_all = pieces.reshape(active_count * active_count, tile_size, tile_size)
    density_all = [density]
    density_out = jnp.stack(density_all, axis=0)
    sending = (
        jnp.zeros((device_count * capacity, tile_size, tile_size), jnp.float32)
        .at[position]
        .set(pieces_all)
    )
    returned = lax.all_to_all(sending, ("row", "col"), split_axis=0, concat_axis=0, tiled=True)
    kept = jnp.where(filled[:, None, None], returned, jnp.float32(0.0))
    h_flat = (
        jnp.zeros((slab_rows * offset_groups, tile_size, tile_size), jnp.float32)
        .at[source]
        .add(kept)
    )
    return (h_flat.reshape(p_tiles.shape), density_out)


def solution(mesh):
    return jax.shard_map(
        local,
        mesh=mesh,
        in_specs=(
            P(None, "row", None, "col", None, None),
            P(),
            P(("row", "col")),
            P(("row", "col"), None, None),
            P(("row", "col"), None),
        ),
        out_specs=(P(None, "row", None, "col", None, None), P(("row", "col"), None)),
        check_vma=False,
    )
```

profile of v0, /device:TPU:5, one launch (start us, length us, event | category | flops | bytes accessed | tf_op | source)
XLA Modules:
  0.0 281.7 jit_solution(13302215753402721199)
XLA Ops:
  0.6 0.7 fusion.22
  1.3 0.7 broadcast_add_fusion
  2.0 0.8 compare_convert_fusion
  2.8 0.1 reduce_window_sum.11
  3.0 0.8 fusion.18
  3.8 6.3 %gather_fusion = bf16[128,128,128]{2,1,0:T(8,128)(2,1)} fusion(f32[128,128,128]{2,1,0:T(8,128)} %bitcast.81, s32[1024]{0:T(1024)S(1)} %pad_clamp_fusion.1), kind=kCustom, calls=%fused_computation | custom fusion | bytes 8389120 | tf_op jit(solution)/shard_map/gather | solution.py:58
  10.1 5.1 %select_convert_fusion = bf16[128,128,128]{2,1,0:T(8,128)(2,1)} fusion(bf16[128,128,128]{2,1,0:T(8,128)(2,1)} %gather_fusion, pred[128]{0:T(512)(128)(4,1)S(1)} %get-tuple-element.2), kind=kLoop, calls=%fused_computation.12 | loop fusion | flops 2097152 | bytes 8388736 | tf_op jit(solution)/shard_map/convert_element_type | solution.py:58
  15.2 11.3 %all-to-all-start = ((bf16[128,128,128]{2,1,0:T(8,128)(2,1)}), bf16[128,128,128]{2,1,0:T(8,128)(2,1)}, u32[]{:S(2)}, u32[]{:S(2)}) async-start(bf16[128,128,128]{2,1,0:T(8,128)(2,1)} %select_convert_fusion), calls=%async_computation | async-start | bytes 8388608 | tf_op jit(solution)/shard_map/all_to_all | solution.py:61
  27.1 11.9 %copy.14 = bf16[1,4096,1024]{1,2,0:T(8,128)(2,1)} copy(bf16[1,4096,1024]{2,1,0:T(8,128)(2,1)} %param.8) | data formatting | bytes 16777216 | tf_op args[3]
  39.1 0.2 dynamic-slice_reduce_fusion
  39.2 0.2 convert_reduce_fusion
  39.4 38.2 %all-to-all-done = bf16[128,128,128]{2,1,0:T(8,128)(2,1)} async-done(((bf16[128,128,128]{2,1,0:T(8,128)(2,1)}), bf16[128,128,128]{2,1,0:T(8,128)(2,1)}, u32[]{:S(2)}, u32[]{:S(2)}) %all-to-all-start) | async-done | bytes 4194336 | tf_op jit(solution)/shard_map/all_to_all | solution.py:61
  77.7 3.1 %gather_fusion.1 = bf16[64,128,128]{2,1,0:T(8,128)(2,1)S(1)} fusion(bf16[128,128,128]{2,1,0:T(8,128)(2,1)} %all-to-all-done, s32[1024]{0:T(1024)S(1)} %pad_clamp_fusion), kind=kCustom, calls=%fused_computation.1 | custom fusion | bytes 4194560 | tf_op jit(solution)/shard_map/gather | solution.py:62
  80.8 0.0 slice-start
  80.8 1.4 copy.13
  82.2 0.0 copy-start
  82.2 0.0 slice-start.1
  82.2 15.0 %fusion = f32[4096]{0:T(1024)S(1)} fusion(bf16[1,4096,1024]{2,1,0:T(8,128)(2,1)} %param.8, bf16[1,4096,1024]{1,2,0:T(8,128)(2,1)} %copy.14, bf16[128,8,8,128]{3,2,1,0:T(8,128)(2,1)S(1)} %bitcast.82), kind=kOutput, calls=%fused_computation.5 | convolution fusion | flops 8602513408 | bytes 18890752 | tf_op jit(solution)/shard_map/dot_general | solution.py:9
  97.3 0.0 copy-done
  97.3 0.0 slice-done
  97.3 0.0 slice-done.1
  97.3 9.6 %fusion.7 = f32[128,8,8,128]{3,1,2,0:T(8,128)S(1)} fusion(bf16[1,4096,1024]{2,1,0:T(8,128)(2,1)S(1)} %bitcast.79, f32[4096]{0:T(1024)S(1)} %select_multiply_fusion), kind=kOutput, calls=%fused_computation.14 | convolution fusion | flops 8602517504 | bytes 12599296 | tf_op jit(solution)/shard_map/dot_general | solution.py:15
  106.9 3.0 %copy.17 = f32[128,8,8,128]{3,2,1,0:T(8,128)} copy(f32[128,8,8,128]{3,1,2,0:T(8,128)S(1)} %fusion.7) | data formatting | bytes 8388608
  110.0 5.4 %copy.15 = f32[8,128,8,128]{3,1,2,0:T(8,128)} copy(f32[8,128,8,128]{1,0,3,2:T(8,128)} %bitcast.77) | data formatting | bytes 8388608 | tf_op jit(solution)/shard_map/reshape | solution.py:67
  115.4 4.5 %broadcast.401.clone = f32[128,128,128]{2,1,0:T(8,128)} broadcast(f32[]{:T(128)} %constant.79.clone.1), dimensions={} | broadcast | bytes 8388612 | tf_op jit(solution)/shard_map/broadcast.8
  119.8 11.8 %scatter_fusion = f32[128,128,128]{2,1,0:T(8,128)} fusion(f32[128,128,128]{2,1,0:T(8,128)} %broadcast.401.clone, s32[64]{0:T(128)S(1)} %fusion.24, f32[64,128,128]{2,1,0:T(8,128)} %bitcast.76), kind=kCustom, calls=%fused_computation.2 | custom fusion | bytes 12583168 | tf_op jit(solution)/shard_map/scatter | solution.py:76
  131.6 5.8 %all-to-all-start.1 = ((f32[128,128,128]{2,1,0:T(8,128)}), f32[128,128,128]{2,1,0:T(8,128)}, u32[]{:S(2)}, u32[]{:S(2)}) async-start(f32[128,128,128]{2,1,0:T(8,128)} %scatter_fusion), calls=%async_computation.1 | async-start | bytes 16777216 | tf_op jit(solution)/shard_map/all_to_all | solution.py:78
  137.5 0.6 compare_select_fusion
  138.1 106.1 %all-to-all-done.1 = f32[128,128,128]{2,1,0:T(8,128)} async-done(((f32[128,128,128]{2,1,0:T(8,128)}), f32[128,128,128]{2,1,0:T(8,128)}, u32[]{:S(2)}, u32[]{:S(2)}) %all-to-all-start.1) | async-done | bytes 8388640 | tf_op jit(solution)/shard_map/all_to_all | solution.py:78
  244.2 7.2 %broadcast_select_fusion = f32[128,128,128]{2,1,0:T(8,128)} fusion(f32[128,128,128]{2,1,0:T(8,128)} %all-to-all-done.1, pred[128]{0:T(512)(128)(4,1)S(1)} %get-tuple-element.2), kind=kLoop, calls=%fused_computation.13 | loop fusion | flops 2097152 | bytes 16777344 | tf_op jit(solution)/shard_map/jit(_where)/select_n | solution.py:79
  251.4 4.5 %broadcast.401 = f32[128,128,128]{2,1,0:T(8,128)} broadcast(f32[]{:T(128)} %constant.79.clone.1), dimensions={} | broadcast | bytes 8388612 | tf_op jit(solution)/shard_map/broadcast.8
  255.9 25.8 %scatter_fusion.1 = f32[128,128,128]{2,1,0:T(8,128)} fusion(f32[128,128,128]{2,1,0:T(8,128)} %broadcast.401, s32[128]{0:T(128)S(1)} %fusion.23, f32[128,128,128]{2,1,0:T(8,128)} %broadcast_select_fusion), kind=kCustom, calls=%fused_computation.3 | custom fusion | flops 2097152 | bytes 25166336 | tf_op jit(solution)/shard_map/scatter-add | solution.py:83
  (7 shorter events, 0.1 us)
Async XLA Ops:
  15.2 62.5 %all-to-all-start = ((bf16[128,128,128]{2,1,0:T(8,128)(2,1)}), bf16[128,128,128]{2,1,0:T(8,128)(2,1)}, u32[]{:S(2)}, u32[]{:S(2)}) async-start(bf16[128,128,128]{2,1,0:T(8,128)(2,1)} %select_convert_fusion), calls=%async_computation | async-start | bytes 8388608 | tf_op jit(solution)/shard_map/all_to_all | solution.py:61
  80.8 16.5 %slice-start = ((s8[8388608]{0:T(1024)(128)(4,1)}), s8[4194304]{0:T(1024)(128)(4,1)S(1)}, s32[]{:S(2)}) async-start(s8[8388608]{0:T(1024)(128)(4,1)} %bitcast.78), calls=%async_computation.2 | async-start | bytes 8388608
  82.2 15.1 %copy-start = (f32[1,4096]{1,0:T(1,128)S(1)}, f32[1,4096]{1,0:T(1,128)}, u32[]{:S(2)}) copy-start(f32[1,4096]{1,0:T(1,128)} %param.9) | copy-start | bytes 49156
  82.2 15.1 %slice-start.1 = ((s8[8388608]{0:T(1024)(128)(4,1)}), s8[4194304]{0:T(1024)(128)(4,1)S(1)}, s32[]{:S(2)}) async-start(s8[8388608]{0:T(1024)(128)(4,1)} %bitcast.78), calls=%async_computation.3 | async-start | bytes 8388608
  131.6 112.6 %all-to-all-start.1 = ((f32[128,128,128]{2,1,0:T(8,128)}), f32[128,128,128]{2,1,0:T(8,128)}, u32[]{:S(2)}, u32[]{:S(2)}) async-start(f32[128,128,128]{2,1,0:T(8,128)} %scatter_fusion), calls=%async_computation.1 | async-start | bytes 16777216 | tf_op jit(solution)/shard_map/all_to_all | solution.py:78
where the time goes:
time: 283 us; the launch traced here: 282 us
  waiting for transfers between devices  144 us (51%)
  local copies, waits for them, and re-layouts  52.1 us (18%)
  other arithmetic  42.1 us (15%)
  matrix products  24.7 us (9%)
  starting transfers between devices  17.1 us (6%)
    all_to_all x1, waiting for transfers between devices, local(): lax.all_to_all(sending, ('row', 'col'), split_axis=0, concat_axis=0, tile...  106 us
    all_to_all x1, waiting for transfers between devices, local(): lax.all_to_all(outgoing, ('row', 'col'), split_axis=0, concat_axis=0, til...  38.2 us
    scatter-add x1, other arithmetic, local(): h_flat = jnp.zeros((slab_rows * offset_groups, tile_size, tile_size), jnp...  25.8 us
    dot_general x1, matrix products, batch_whole(): product = jnp.dot(values, matrix, preferred_element_type=jnp.float32)  15 us
    unnamed x8, local copies, waits for them, and re-layouts  15 us
    scatter x1, local copies, waits for them, and re-layouts, local(): sending = jnp.zeros((device_count * capacity, tile_size, tile_size), jnp....  11.8 us
    all_to_all x1, starting transfers between devices, local(): lax.all_to_all(outgoing, ('row', 'col'), split_axis=0, concat_axis=0, til...  11.3 us
    dot_general x1, matrix products, batch_whole(): lax.dot_general(values, weighted, (((0,), (0,)), ((), ())), preferred_ele...  9.61 us
  transfers between devices with their start and end apart: 2, of which 2 were waited for; matrix products, arithmetic and copies ran while one was open for 5% of the time, Pallas kernels for 0%

commit v1 on v0

v1 whole, which is shorter than its diff:
```python
import functools

import jax
import jax.numpy as jnp
from jax import lax
from jax.experimental import pallas as pl
from jax.experimental.pallas import tpu as pltpu
from jax.sharding import PartitionSpec as P

MESH = pl.DeviceIdType.MESH
TILE = 128
ACT = 8
PTS = 4096
SPAN = ACT * TILE
ROWS = 8
COLS = 16
DEV = ROWS * COLS
PLACES = 128
CHUNKS = 4
CROWS = TILE // CHUNKS
UNUSED = 8
PT = 512


def exchange_kernel(
    act, cnt, kern, p_hbm, basis_hbm, dens, hrecv, table,
    p_buf, s_buf, r_buf, basis, basis_t, p_chunk, weighted, h_send, kd, slots,
    p_sem, b_sem, send_sem, recv_sem, hsend_sem, hrecv_sem, own_sem,
):
    r = lax.axis_index("row")
    c = lax.axis_index("col")
    me = r * COLS + c

    def p_copy(q):
        return pltpu.make_async_copy(p_hbm.at[:, pl.ds(q * CROWS, CROWS), :], p_buf[q], p_sem.at[q])

    def basis_copy(i):
        return pltpu.make_async_copy(basis_hbm.at[:, pl.ds(i * TILE, TILE)], basis.at[i], b_sem.at[i])

    for q in range(CHUNKS):
        p_copy(q).start()
    for i in range(ACT):
        basis_copy(i).start()

    barrier = pltpu.get_barrier_semaphore()

    def greet(d, carry):
        t = (me + d) % DEV
        pl.semaphore_signal(barrier, inc=1, device_id=(t // COLS, t % COLS), device_id_type=MESH)
        return carry

    lax.fori_loop(1, DEV, greet, 0)

    def find(n, carry):
        first = act[n * ACT]
        i = (r - first) & 7
        a = act[n * ACT + i]
        b = act[n * ACT + ((i + c) & 7)]
        o = (b - a + 2 * ACT) & 511
        place = (a >> 3) * 2 + ((o >> 4) & 1)
        table[n] = jnp.where((o & 15) == c, place, -1)
        return carry

    lax.fori_loop(0, DEV, find, 0)

    start = act[me * ACT]

    def find_slot(e, carry):
        ri = e // ACT
        rj = e % ACT
        a = act[me * ACT + ((ri - start) & 7)]
        b = act[me * ACT + ((rj - start) & 7)]
        slots[e] = ri * COLS + ((b - a + 2 * ACT) & 15)
        return carry

    lax.fori_loop(0, ACT * ACT, find_slot, 0)

    pl.semaphore_wait(barrier, DEV - 1)

    for q in range(CHUNKS):
        p_copy(q).wait()

        def pack(t, q=q):
            place = jnp.maximum(table[t], 0)
            s_buf[q][t] = p_buf[q][place].astype(jnp.bfloat16)

        @pl.when(c != UNUSED)
        def _(q=q, pack=pack):
            def send(d, carry):
                e = (d * 27) % DEV
                tr = (r + e // COLS) % ROWS
                tc = (c + e % COLS) % COLS
                t = tr * COLS + tc
                pack(t)
                pltpu.make_async_remote_copy(
                    src_ref=s_buf[q].at[t],
                    dst_ref=r_buf[q].at[me],
                    send_sem=send_sem.at[q],
                    recv_sem=recv_sem.at[q],
                    device_id=(tr, tc),
                    device_id_type=MESH,
                ).start()
                return carry

            lax.fori_loop(1, DEV, send, 0)
            pack(me)
            r_buf[q][me] = s_buf[q][me]

    for i in range(ACT):
        basis_copy(i).wait()
    for rho in range(ACT):
        block = (rho - start) & 7

        def turn(m, carry, rho=rho, block=block):
            rows = pl.ds(pl.multiple_of(m * PT, PT), PT)
            basis_t[rho, :, rows] = basis[block, rows, :].T
            return carry

        lax.fori_loop(0, PTS // PT, turn, 0)

    dens[...] = jnp.zeros_like(dens)
    for q in range(CHUNKS):
        for total, is_here in ((DEV - ROWS, c == UNUSED), (DEV - ROWS - 1, c != UNUSED)):
            @pl.when(is_here)
            def _(q=q, total=total):
                ref = r_buf[q].at[pl.ds(0, total)]
                pltpu.make_async_copy(ref, ref, recv_sem.at[q]).wait()

        def place_rows(ri, carry, q=q):
            for rj in range(ACT):
                p_chunk[ri, :, rj * TILE : (rj + 1) * TILE] = r_buf[q][slots[ri * ACT + rj]]
            return carry

        lax.fori_loop(0, ACT, place_rows, 0)

        def density_part(m, carry, q=q):
            cols = pl.ds(pl.multiple_of(m * PT, PT), PT)
            prod = jnp.dot(
                p_chunk[...].reshape(ACT * CROWS, SPAN),
                basis_t[:, :, cols].reshape(SPAN, PT),
                preferred_element_type=jnp.float32,
            )
            left = basis_t[:, q * CROWS : (q + 1) * CROWS, cols].reshape(ACT * CROWS, PT)
            dens[:, cols] += jnp.sum(prod * left.astype(jnp.float32), axis=0, keepdims=True)
            return carry

        lax.fori_loop(0, PTS // PT, density_part, 0)

    point = lax.broadcasted_iota(jnp.int32, (1, PTS), 1)
    masked = jnp.where(point < cnt[0], dens[...], 0.0)
    dens[...] = masked
    kd[...] = kern[...] * masked

    own_copy = pltpu.make_async_copy(h_send.at[0, 0], hrecv.at[me], own_sem)

    def hamilton_step(step, carry):
        pair = (step + c + c // 4) % 4

        def weigh(m, carry):
            cols = pl.ds(pl.multiple_of(m * PT, PT), PT)
            values = basis_t[pl.ds(2 * pair, 2), :, cols].reshape(2 * TILE, PT).astype(jnp.float32)
            weighted[:, cols] = (values * kd[:, cols]).astype(jnp.bfloat16)
            return carry

        lax.fori_loop(0, PTS // PT, weigh, 0)

        def part(turn_of, carry):
            m = (turn_of + r // 2 + 2 * (r % 2) + c + c // 4) % 4
            two = [basis[(2 * m + ii - start) & 7] for ii in range(2)]
            x = jnp.dot(weighted[...], jnp.concatenate(two, axis=1), preferred_element_type=jnp.float32)
            for ii in range(2):
                for jj in range(2):
                    tile = x[jj * TILE : (jj + 1) * TILE, ii * TILE : (ii + 1) * TILE]
                    h_send[2 * m + ii, 2 * pair + jj] = tile.T.astype(jnp.bfloat16)
            for ii in range(2):
                give(2 * m + ii)
            return carry

        def give(ri):
            for jj in range(2):
                rj = 2 * pair + jj
                c8 = (rj - ri + ACT) % ACT
                for half in range(2):
                    tc = c8 + half * ACT
                    is_me = jnp.logical_and(ri == r, tc == c)

                    @pl.when(jnp.logical_and(tc != UNUSED, is_me))
                    def _():
                        pltpu.make_async_copy(h_send.at[ri, rj], hrecv.at[me], own_sem).start()

                    @pl.when(jnp.logical_and(tc != UNUSED, jnp.logical_not(is_me)))
                    def _():
                        pltpu.make_async_remote_copy(
                            src_ref=h_send.at[ri, rj],
                            dst_ref=hrecv.at[me],
                            send_sem=hsend_sem,
                            recv_sem=hrecv_sem,
                            device_id=(ri, tc),
                            device_id_type=MESH,
                        ).start()

        lax.fori_loop(0, ACT // 2, part, 0)
        return carry

    lax.fori_loop(0, 4, hamilton_step, 0)

    @pl.when(c != UNUSED)
    def _():
        for q in range(CHUNKS):
            sent = s_buf[q].at[pl.ds(0, DEV - 1)]
            pltpu.make_async_copy(sent, sent, send_sem.at[q]).wait()
        own_copy.wait()
        sent = hrecv.at[pl.ds(0, DEV - ROWS - 1)]
        pltpu.make_async_copy(sent, sent, hsend_sem).wait()
        came = hrecv.at[pl.ds(0, DEV - 1)]
        pltpu.make_async_copy(came, came, hrecv_sem).wait()

    @pl.when(c == UNUSED)
    def _():
        sent = hrecv.at[pl.ds(0, DEV - ROWS)]
        pltpu.make_async_copy(sent, sent, hsend_sem).wait()


def exchange(act, cnt, kern, p, basis):
    any_space = pl.BlockSpec(memory_space=pl.ANY)
    smem = pl.BlockSpec(memory_space=pltpu.SMEM)
    vmem = pl.BlockSpec(memory_space=pltpu.VMEM)
    chunk = lambda dtype: [pltpu.VMEM((DEV, CROWS, TILE), dtype) for _ in range(CHUNKS)]
    return pl.pallas_call(
        exchange_kernel,
        out_shape=(
            jax.ShapeDtypeStruct((1, PTS), jnp.float32),
            jax.ShapeDtypeStruct((DEV, TILE, TILE), jnp.bfloat16),
            jax.ShapeDtypeStruct((DEV,), jnp.int32),
        ),
        in_specs=[smem, smem, vmem, any_space, any_space],
        out_specs=(vmem, any_space, smem),
        scratch_shapes=[
            chunk(jnp.float32),
            chunk(jnp.bfloat16),
            chunk(jnp.bfloat16),
            pltpu.VMEM((ACT, PTS, TILE), jnp.bfloat16),
            pltpu.VMEM((ACT, TILE, PTS), jnp.bfloat16),
            pltpu.VMEM((ACT, CROWS, SPAN), jnp.bfloat16),
            pltpu.VMEM((2 * TILE, PTS), jnp.bfloat16),
            pltpu.VMEM((ACT, ACT, TILE, TILE), jnp.bfloat16),
            pltpu.VMEM((1, PTS), jnp.float32),
            pltpu.SMEM((ACT * ACT,), jnp.int32),
            pltpu.SemaphoreType.DMA((CHUNKS,)),
            pltpu.SemaphoreType.DMA((ACT,)),
            pltpu.SemaphoreType.DMA((CHUNKS,)),
            pltpu.SemaphoreType.DMA((CHUNKS,)),
            pltpu.SemaphoreType.DMA,
            pltpu.SemaphoreType.DMA,
            pltpu.SemaphoreType.DMA,
        ],
        compiler_params=pltpu.CompilerParams(
            collective_id=0, has_side_effects=True, vmem_limit_bytes=56 * 2**20
        ),
    )(act, cnt, kern, p, basis)


def scatter_kernel(table, came, out):
    out[...] = jnp.zeros_like(out)

    def add(n, carry):
        place = table[n]

        @pl.when(place >= 0)
        def _():
            out[place] += came[n].astype(jnp.float32)

        return carry

    lax.fori_loop(0, DEV, add, 0)


def scatter(table, came):
    parts = 2
    rows = TILE // parts
    return pl.pallas_call(
        scatter_kernel,
        grid=(parts,),
        out_shape=jax.ShapeDtypeStruct((PLACES, TILE, TILE), jnp.float32),
        in_specs=[
            pl.BlockSpec(memory_space=pltpu.SMEM),
            pl.BlockSpec((DEV, rows, TILE), lambda g: (0, g, 0)),
        ],
        out_specs=pl.BlockSpec((PLACES, rows, TILE), lambda g: (0, g, 0)),
        compiler_params=pltpu.CompilerParams(vmem_limit_bytes=40 * 2**20),
    )(table, came)


def local(p_tiles, active, counts, basis, kernel):
    dens, came, table = exchange(
        active.reshape(DEV * ACT),
        counts,
        kernel,
        p_tiles.reshape(PLACES, TILE, TILE),
        basis.reshape(PTS, SPAN),
    )
    return scatter(table, came).reshape(p_tiles.shape), dens


def solution(mesh):
    return jax.shard_map(
        local,
        mesh=mesh,
        in_specs=(
            P(None, "row", None, "col", None, None),
            P(),
            P(("row", "col")),
            P(("row", "col"), None, None),
            P(("row", "col"), None),
        ),
        out_specs=(P(None, "row", None, "col", None, None), P(("row", "col"), None)),
        check_vma=False,
    )
```

time: 283 us -> 134 us (0.47)
  the two profiles are of different devices: /device:TPU:5 before, /device:TPU:1 now
where the time goes in v1:
time: 134 us; the launch traced here: 133 us
  Pallas kernels  127 us (95%)
  local copies, waits for them, and re-layouts  4.92 us (4%)
    pallas_call x1, Pallas kernels, exchange(): pl.pallas_call(exchange_kernel, out_shape=(jax.ShapeDtypeStruct((1, PTS),...  120 us
    pallas_call x1, Pallas kernels, scatter(): pl.pallas_call(scatter_kernel, grid=(parts,), out_shape=jax.ShapeDtypeStr...  7.45 us
    unnamed x8, local copies, waits for them, and re-layouts  4.24 us

profile of v1, /device:TPU:1, one launch (start us, length us, event | category | flops | bytes accessed | tf_op | source)
XLA Modules:
  0.0 133.3 jit_solution(7493269637692445457)
XLA Ops:
  1.3 0.8 copy.8
  2.1 0.7 reshape.16.act
  2.7 119.6 %shard_map.68 = (f32[1,4096]{1,0:T(1,128)}, bf16[128,128,128]{2,1,0:T(8,128)(2,1)}, s32[128]{0:T(128)}) custom-call(s32[1024]{0:T(1024)} %reshape.16.act, s32[1]{0:T(128)S(6)} %copy.11.cnt, f32[1,4096]{1,0:T(1,128)} %kern.1, f32[128,128,128]{2,1,0:T(8,128)} %bitcast.5, bf16[4096,1024]{1,0:T(8,128)(2,1)} %bitcast.6), custom_call_target="tpu_custom_call" | custom-call | tf_op jit(solution)/shard_map/pallas_call | solution.py:229
  122.4 0.0 copy-start
  122.4 2.2 %copy-done = bf16[128,128,128]{2,1,0:T(8,128)(2,1)S(1)} copy-done((bf16[128,128,128]{2,1,0:T(8,128)(2,1)S(1)}, bf16[128,128,128]{2,1,0:T(8,128)(2,1)}, u32[]{:S(2)}) %copy-start) | copy-done | bytes 4194328
  124.5 0.0 copy-start.1
  124.6 0.7 copy-done.1
  125.2 0.0 copy-start.2
  125.2 7.5 %shard_map.69 = f32[128,128,128]{2,1,0:T(8,128)} custom-call(s32[128]{0:T(128)S(1)} %copy-done.1, bf16[128,128,128]{2,1,0:T(8,128)(2,1)S(1)} %copy-done), custom_call_target="tpu_custom_call" | custom-call | tf_op jit(solution)/shard_map/pallas_call | solution.py:281
  132.7 0.0 copy-done.2
  132.7 0.6 copy.12
Async XLA Ops:
  122.4 2.2 %copy-start = (bf16[128,128,128]{2,1,0:T(8,128)(2,1)S(1)}, bf16[128,128,128]{2,1,0:T(8,128)(2,1)}, u32[]{:S(2)}) copy-start(bf16[128,128,128]{2,1,0:T(8,128)(2,1)} %get-tuple-element.6.came) | copy-start | bytes 12582916
  124.5 0.7 copy-start.1
  125.2 7.5 %copy-start.2 = (f32[1,4096]{1,0:T(1,128)S(1)}, f32[1,4096]{1,0:T(1,128)}, u32[]{:S(2)}) copy-start(f32[1,4096]{1,0:T(1,128)} %get-tuple-element.15) | copy-start | bytes 49156

commit v2 on v1

--- a/solution.py
+++ b/solution.py
@@ -16,23 +16,30 @@
 COLS = 16
 DEV = ROWS * COLS
 PLACES = 128
-CHUNKS = 4
-CROWS = TILE // CHUNKS
+SIZES = (48, 32, 32, 16)
+FIRST = (0, 48, 80, 112)
+CHUNKS = len(SIZES)
+CROWS = 32
+PARTS = TILE // CROWS
+MIX = 23
+EARLY = 1
 UNUSED = 8
 PT = 512
+DPT = 1024
+UNROLL = 4
 
 
 def exchange_kernel(
     act, cnt, kern, p_hbm, basis_hbm, dens, hrecv, table,
     p_buf, s_buf, r_buf, basis, basis_t, p_chunk, weighted, h_send, kd, slots,
-    p_sem, b_sem, send_sem, recv_sem, hsend_sem, hrecv_sem, own_sem,
+    p_sem, b_sem, send_sem, recv_sem, hsend_sem, hrecv_sem, own_sem, all_sem,
 ):
     r = lax.axis_index("row")
     c = lax.axis_index("col")
     me = r * COLS + c
 
     def p_copy(q):
-        return pltpu.make_async_copy(p_hbm.at[:, pl.ds(q * CROWS, CROWS), :], p_buf[q], p_sem.at[q])
+        return pltpu.make_async_copy(p_hbm.at[:, pl.ds(FIRST[q], SIZES[q]), :], p_buf[q], p_sem.at[q])
 
     def basis_copy(i):
         return pltpu.make_async_copy(basis_hbm.at[:, pl.ds(i * TILE, TILE)], basis.at[i], b_sem.at[i])
@@ -44,18 +51,21 @@
 
     barrier = pltpu.get_barrier_semaphore()
 
-    def greet(d, carry):
-        t = (me + d) % DEV
-        pl.semaphore_signal(barrier, inc=1, device_id=(t // COLS, t % COLS), device_id_type=MESH)
-        return carry
-
-    lax.fori_loop(1, DEV, greet, 0)
+    def row_peer(d):
+        return lax.rem(r + d, ROWS), c
+
+    def col_peer(d):
+        return r, lax.rem(c + d, COLS)
+
+    for d in range(1, ROWS):
+        pl.semaphore_signal(barrier, inc=1, device_id=row_peer(d), device_id_type=MESH)
+    for d in range(1, COLS):
+        pl.semaphore_signal(barrier, inc=1, device_id=col_peer(d), device_id_type=MESH)
 
     def find(n, carry):
-        first = act[n * ACT]
-        i = (r - first) & 7
-        a = act[n * ACT + i]
-        b = act[n * ACT + ((i + c) & 7)]
+        i = (r - act[0, n]) & 7
+        a = act[i, n]
+        b = act[(i + c) & 7, n]
         o = (b - a + 2 * ACT) & 511
         place = (a >> 3) * 2 + ((o >> 4) & 1)
         table[n] = jnp.where((o & 15) == c, place, -1)
@@ -63,47 +73,78 @@
 
     lax.fori_loop(0, DEV, find, 0)
 
-    start = act[me * ACT]
+    start = act[0, me]
 
     def find_slot(e, carry):
         ri = e // ACT
         rj = e % ACT
-        a = act[me * ACT + ((ri - start) & 7)]
-        b = act[me * ACT + ((rj - start) & 7)]
+        a = act[(ri - start) & 7, me]
+        b = act[(rj - start) & 7, me]
         slots[e] = ri * COLS + ((b - a + 2 * ACT) & 15)
         return carry
 
     lax.fori_loop(0, ACT * ACT, find_slot, 0)
 
-    pl.semaphore_wait(barrier, DEV - 1)
-
+    pl.semaphore_wait(barrier, ROWS + COLS - 2)
+    for d in range(1, ROWS):
+        pl.semaphore_signal(all_sem, inc=1, device_id=row_peer(d), device_id_type=MESH)
+
+    def pack(q, t):
+        place = jnp.maximum(table[t], 0)
+        s_buf[q][t] = p_buf[q][place].astype(jnp.bfloat16)
+
+    def send(q, tr, tc):
+        t = tr * COLS + tc
+        pack(q, t)
+        pltpu.make_async_remote_copy(
+            src_ref=s_buf[q].at[t],
+            dst_ref=r_buf[q].at[me],
+            send_sem=send_sem.at[q],
+            recv_sem=recv_sem.at[q],
+            device_id=(tr, tc),
+            device_id_type=MESH,
+        ).start()
+
+    def send_to_peers(q):
+        def to_row(d, carry):
+            send(q, *row_peer(d))
+            return carry
+
+        def to_col(d, carry):
+            send(q, *col_peer(d))
+            return carry
+
+        lax.fori_loop(1, ROWS, to_row, 0)
+        lax.fori_loop(1, COLS, to_col, 0)
+
+    def send_to_others(q):
+        others = (ROWS - 1) * (COLS - 1)
+
+        def to_other(d, carry):
+            e = lax.rem(d * MIX, others)
+            send(q, row_peer(1 + lax.div(e, COLS - 1))[0], col_peer(1 + lax.rem(e, COLS - 1))[1])
+            return carry
+
+        lax.fori_loop(0, others, to_other, 0)
+
+    for q in range(EARLY):
+        p_copy(q).wait()
+
+        @pl.when(c != UNUSED)
+        def _(q=q):
+            send_to_peers(q)
+
+    pl.semaphore_wait(all_sem, ROWS - 1)
     for q in range(CHUNKS):
-        p_copy(q).wait()
-
-        def pack(t, q=q):
-            place = jnp.maximum(table[t], 0)
-            s_buf[q][t] = p_buf[q][place].astype(jnp.bfloat16)
+        if q >= EARLY:
+            p_copy(q).wait()
 
         @pl.when(c != UNUSED)
-        def _(q=q, pack=pack):
-            def send(d, carry):
-                e = (d * 27) % DEV
-                tr = (r + e // COLS) % ROWS
-                tc = (c + e % COLS) % COLS
-                t = tr * COLS + tc
-                pack(t)
-                pltpu.make_async_remote_copy(
-                    src_ref=s_buf[q].at[t],
-                    dst_ref=r_buf[q].at[me],
-                    send_sem=send_sem.at[q],
-                    recv_sem=recv_sem.at[q],
-                    device_id=(tr, tc),
-                    device_id_type=MESH,
-                ).start()
-                return carry
-
-            lax.fori_loop(1, DEV, send, 0)
-            pack(me)
+        def _(q=q):
+            if q >= EARLY:
+                send_to_peers(q)
+            send_to_others(q)
+            pack(q, me)
             r_buf[q][me] = s_buf[q][me]
 
     for i in range(ACT):
@@ -128,23 +169,23 @@
 
         def place_rows(ri, carry, q=q):
             for rj in range(ACT):
-                p_chunk[ri, :, rj * TILE : (rj + 1) * TILE] = r_buf[q][slots[ri * ACT + rj]]
+                p_chunk[q][ri, :, rj * TILE : (rj + 1) * TILE] = r_buf[q][slots[ri * ACT + rj]]
             return carry
 
         lax.fori_loop(0, ACT, place_rows, 0)
 
         def density_part(m, carry, q=q):
-            cols = pl.ds(pl.multiple_of(m * PT, PT), PT)
+            cols = pl.ds(pl.multiple_of(m * DPT, DPT), DPT)
             prod = jnp.dot(
-                p_chunk[...].reshape(ACT * CROWS, SPAN),
-                basis_t[:, :, cols].reshape(SPAN, PT),
+                p_chunk[q][...].reshape(ACT * SIZES[q], SPAN),
+                basis_t[:, :, cols].reshape(SPAN, DPT),
                 preferred_element_type=jnp.float32,
             )
-            left = basis_t[:, q * CROWS : (q + 1) * CROWS, cols].reshape(ACT * CROWS, PT)
+            left = basis_t[:, FIRST[q] : FIRST[q] + SIZES[q], cols].reshape(ACT * SIZES[q], DPT)
             dens[:, cols] += jnp.sum(prod * left.astype(jnp.float32), axis=0, keepdims=True)
             return carry
 
-        lax.fori_loop(0, PTS // PT, density_part, 0)
+        lax.fori_loop(0, PTS // DPT, density_part, 0)
 
     point = lax.broadcasted_iota(jnp.int32, (1, PTS), 1)
     masked = jnp.where(point < cnt[0], dens[...], 0.0)
@@ -225,7 +266,7 @@
     any_space = pl.BlockSpec(memory_space=pl.ANY)
     smem = pl.BlockSpec(memory_space=pltpu.SMEM)
     vmem = pl.BlockSpec(memory_space=pltpu.VMEM)
-    chunk = lambda dtype: [pltpu.VMEM((DEV, CROWS, TILE), dtype) for _ in range(CHUNKS)]
+    chunk = lambda dtype: [pltpu.VMEM((DEV, rows, TILE), dtype) for rows in SIZES]
     return pl.pallas_call(
         exchange_kernel,
         out_shape=(
@@ -241,7 +282,7 @@
             chunk(jnp.bfloat16),
             pltpu.VMEM((ACT, PTS, TILE), jnp.bfloat16),
             pltpu.VMEM((ACT, TILE, PTS), jnp.bfloat16),
-            pltpu.VMEM((ACT, CROWS, SPAN), jnp.bfloat16),
+            [pltpu.VMEM((ACT, rows, SPAN), jnp.bfloat16) for rows in SIZES],
             pltpu.VMEM((2 * TILE, PTS), jnp.bfloat16),
             pltpu.VMEM((ACT, ACT, TILE, TILE), jnp.bfloat16),
             pltpu.VMEM((1, PTS), jnp.float32),
@@ -253,6 +294,7 @@
             pltpu.SemaphoreType.DMA,
             pltpu.SemaphoreType.DMA,
             pltpu.SemaphoreType.DMA,
+            pltpu.SemaphoreType.REGULAR,
         ],
         compiler_params=pltpu.CompilerParams(
             collective_id=0, has_side_effects=True, vmem_limit_bytes=56 * 2**20
@@ -260,46 +302,85 @@
     )(act, cnt, kern, p, basis)
 
 
-def scatter_kernel(table, came, out):
-    out[...] = jnp.zeros_like(out)
-
-    def add(n, carry):
+def scatter_kernel(table, dens, came, out, dens_out, c_buf, o_buf, which, where, in_sem, out_sem):
+    def take(g):
+        return pltpu.make_async_copy(came.at[:, pl.ds(g * CROWS, CROWS), :], c_buf.at[g], in_sem.at[g])
+
+    def put(g):
+        return pltpu.make_async_copy(
+            o_buf.at[g, pl.ds(0, PLACES)], out.at[:, pl.ds(g * CROWS, CROWS), :], out_sem.at[g]
+        )
+
+    for g in range(PARTS):
+        take(g).start()
+    dens_out[...] = dens[...]
+
+    def compact(n, count):
         place = table[n]
-
-        @pl.when(place >= 0)
-        def _():
-            out[place] += came[n].astype(jnp.float32)
-
-        return carry
-
-    lax.fori_loop(0, DEV, add, 0)
-
-
-def scatter(table, came):
-    parts = 2
-    rows = TILE // parts
+        which[count] = n
+        where[count] = place
+        return count + (place >= 0).astype(jnp.int32)
+
+    count = lax.fori_loop(0, DEV, compact, 0)
+    for e in range(UNROLL - 1):
+        which[count + e] = 0
+        where[count + e] = PLACES
+    rounds = (count + UNROLL - 1) // UNROLL
+
+    for g in range(PARTS):
+
+        def clear(n, carry, g=g):
+            o_buf[g, pl.ds(n * 8, 8)] = jnp.zeros((8, CROWS, TILE), jnp.float32)
+            return carry
+
+        lax.fori_loop(0, PLACES // 8, clear, 0)
+        take(g).wait()
+
+        def add(m, carry, g=g):
+            for e in range(UNROLL):
+                o_buf[g, where[m * UNROLL + e]] += c_buf[g, which[m * UNROLL + e]].astype(jnp.float32)
+            return carry
+
+        lax.fori_loop(0, rounds, add, 0)
+        put(g).start()
+    for g in range(PARTS):
+        put(g).wait()
+
+
+def scatter(table, dens, came):
+    any_space = pl.BlockSpec(memory_space=pl.ANY)
+    smem = pl.BlockSpec(memory_space=pltpu.SMEM)
+    vmem = pl.BlockSpec(memory_space=pltpu.VMEM)
     return pl.pallas_call(
         scatter_kernel,
-        grid=(parts,),
-        out_shape=jax.ShapeDtypeStruct((PLACES, TILE, TILE), jnp.float32),
-        in_specs=[
-            pl.BlockSpec(memory_space=pltpu.SMEM),
-            pl.BlockSpec((DEV, rows, TILE), lambda g: (0, g, 0)),
+        out_shape=(
+            jax.ShapeDtypeStruct((PLACES, TILE, TILE), jnp.float32),
+            jax.ShapeDtypeStruct((1, PTS), jnp.float32),
+        ),
+        in_specs=[smem, vmem, any_space],
+        out_specs=(any_space, vmem),
+        scratch_shapes=[
+            pltpu.VMEM((PARTS, DEV, CROWS, TILE), jnp.bfloat16),
+            pltpu.VMEM((PARTS, PLACES + 1, CROWS, TILE), jnp.float32),
+            pltpu.SMEM((DEV + UNROLL,), jnp.int32),
+            pltpu.SMEM((DEV + UNROLL,), jnp.int32),
+            pltpu.SemaphoreType.DMA((PARTS,)),
+            pltpu.SemaphoreType.DMA((PARTS,)),
         ],
-        out_specs=pl.BlockSpec((PLACES, rows, TILE), lambda g: (0, g, 0)),
-        compiler_params=pltpu.CompilerParams(vmem_limit_bytes=40 * 2**20),
-    )(table, came)
+        compiler_params=pltpu.CompilerParams(vmem_limit_bytes=60 * 2**20),
+    )(table, dens, came)
 
 
 def local(p_tiles, active, counts, basis, kernel):
     dens, came, table = exchange(
-        active.reshape(DEV * ACT),
+        active.T,
         counts,
         kernel,
         p_tiles.reshape(PLACES, TILE, TILE),
         basis.reshape(PTS, SPAN),
     )
-    return scatter(table, came).reshape(p_tiles.shape), dens
+    h_tiles, dens = scatter(table, dens, came)
+    return h_tiles.reshape(p_tiles.shape), dens
 
 
 def solution(mesh):

time: 134 us -> 122 us (0.910)
  Pallas kernels: 127 us -> 121 us
  local copies, waits for them, and re-layouts: 4.92 us -> 0 us
    pallas_call x1, Pallas kernels: 120 us -> 114 us  [exchange(): pl.pallas_call(exchange_kernel, out_shape=(jax.ShapeDtypeStruct((1, PTS),...]
    unnamed x8 -> x0, local copies, waits for them, and re-layouts: 4.24 us -> none
where the time goes in v2:
time: 122 us
  Pallas kernels  121 us (99%)
  between operations  1.28 us (1%)
    pallas_call x1, Pallas kernels, exchange(): pl.pallas_call(exchange_kernel, out_shape=(jax.ShapeDtypeStruct((1, PTS),...  114 us
    pallas_call x1, Pallas kernels, scatter(): pl.pallas_call(scatter_kernel, out_shape=(jax.ShapeDtypeStruct((PLACES, T...  6.96 us

profile of v2, /device:TPU:1, one launch (start us, length us, event | category | flops | bytes accessed | tf_op | source)
XLA Modules:
  0.0 121.9 jit_solution(10709973505087004994)
XLA Ops:
  1.3 113.6 %shard_map.68 = (f32[1,4096]{1,0:T(1,128)}, bf16[128,128,128]{2,1,0:T(8,128)(2,1)}, s32[128]{0:T(128)}) custom-call(s32[8,128]{1,0:T(8,128)} %bitcast.8, s32[1]{0:T(128)S(6)} %copy.8.cnt, f32[1,4096]{1,0:T(1,128)} %kern.1, f32[128,128,128]{2,1,0:T(8,128)} %bitcast.6, bf16[4096,1024]{1,0:T(8,128)(2,1)} %bitcast.7), custom_call_target="tpu_custom_call" | custom-call | tf_op jit(solution)/shard_map/pallas_call | solution.py:270
  114.9 7.0 %shard_map.69 = (f32[128,128,128]{2,1,0:T(8,128)}, f32[1,4096]{1,0:T(1,128)}) custom-call(s32[128]{0:T(128)} %get-tuple-element.7.table, f32[1,4096]{1,0:T(1,128)} %get-tuple-element.8.dens, bf16[128,128,128]{2,1,0:T(8,128)(2,1)} %get-tuple-element.9.came), custom_call_target="tpu_custom_call" | custom-call | tf_op jit(solution)/shard_map/pallas_call | solution.py:354

commit v3 on v2

--- a/solution.py
+++ b/solution.py
@@ -30,9 +30,9 @@
 
 
 def exchange_kernel(
-    act, cnt, kern, p_hbm, basis_hbm, dens, hrecv, table,
-    p_buf, s_buf, r_buf, basis, basis_t, p_chunk, weighted, h_send, kd, slots,
-    p_sem, b_sem, send_sem, recv_sem, hsend_sem, hrecv_sem, own_sem, all_sem,
+    act_hbm, cnt_hbm, kern_hbm, p_hbm, basis_hbm, dens_hbm, hrecv, table_hbm,
+    act, cnt, kern, dens, table, p_buf, s_buf, r_buf, basis, basis_t, p_chunk, weighted, h_send, kd, slots,
+    p_sem, b_sem, send_sem, recv_sem, hsend_sem, hrecv_sem, own_sem, all_sem, small_sem,
 ):
     r = lax.axis_index("row")
     c = lax.axis_index("col")
@@ -44,23 +44,32 @@
     def basis_copy(i):
         return pltpu.make_async_copy(basis_hbm.at[:, pl.ds(i * TILE, TILE)], basis.at[i], b_sem.at[i])
 
+    barrier = pltpu.get_barrier_semaphore()
+
+    def row_peer(d):
+        return lax.rem(r + d, ROWS), c
+
+    def col_peer(d):
+        return r, lax.rem(c + d, COLS)
+
+    for d in range(1, ROWS):
+        pl.semaphore_signal(barrier, inc=1, device_id=row_peer(d), device_id_type=MESH)
+    for d in range(1, COLS):
+        pl.semaphore_signal(barrier, inc=1, device_id=col_peer(d), device_id_type=MESH)
+
+    act_copy = pltpu.make_async_copy(act_hbm, act, small_sem.at[0])
+    cnt_copy = pltpu.make_async_copy(cnt_hbm, cnt, small_sem.at[1])
+    kern_copy = pltpu.make_async_copy(kern_hbm, kern, small_sem.at[2])
+    table_copy = pltpu.make_async_copy(table, table_hbm, small_sem.at[3])
+    dens_copy = pltpu.make_async_copy(dens, dens_hbm, small_sem.at[4])
+    act_copy.start()
     for q in range(CHUNKS):
         p_copy(q).start()
     for i in range(ACT):
         basis_copy(i).start()
-
-    barrier = pltpu.get_barrier_semaphore()
-
-    def row_peer(d):
-        return lax.rem(r + d, ROWS), c
-
-    def col_peer(d):
-        return r, lax.rem(c + d, COLS)
-
-    for d in range(1, ROWS):
-        pl.semaphore_signal(barrier, inc=1, device_id=row_peer(d), device_id_type=MESH)
-    for d in range(1, COLS):
-        pl.semaphore_signal(barrier, inc=1, device_id=col_peer(d), device_id_type=MESH)
+    cnt_copy.start()
+    kern_copy.start()
+    act_copy.wait()
 
     def find(n, carry):
         i = (r - act[0, n]) & 7
@@ -72,6 +81,7 @@
         return carry
 
     lax.fori_loop(0, DEV, find, 0)
+    table_copy.start()
 
     start = act[0, me]
 
@@ -187,15 +197,18 @@
 
         lax.fori_loop(0, PTS // DPT, density_part, 0)
 
+    cnt_copy.wait()
+    kern_copy.wait()
     point = lax.broadcasted_iota(jnp.int32, (1, PTS), 1)
     masked = jnp.where(point < cnt[0], dens[...], 0.0)
     dens[...] = masked
+    dens_copy.start()
     kd[...] = kern[...] * masked
 
     own_copy = pltpu.make_async_copy(h_send.at[0, 0], hrecv.at[me], own_sem)
 
     def hamilton_step(step, carry):
-        pair = (step + c + c // 4) % 4
+        pair = (step + r // 2 + c // 4) % 4
 
         def weigh(m, carry):
             cols = pl.ds(pl.multiple_of(m * PT, PT), PT)
@@ -245,6 +258,9 @@
 
     lax.fori_loop(0, 4, hamilton_step, 0)
 
+    table_copy.wait()
+    dens_copy.wait()
+
     @pl.when(c != UNUSED)
     def _():
         for q in range(CHUNKS):
@@ -264,8 +280,6 @@
 
 def exchange(act, cnt, kern, p, basis):
     any_space = pl.BlockSpec(memory_space=pl.ANY)
-    smem = pl.BlockSpec(memory_space=pltpu.SMEM)
-    vmem = pl.BlockSpec(memory_space=pltpu.VMEM)
     chunk = lambda dtype: [pltpu.VMEM((DEV, rows, TILE), dtype) for rows in SIZES]
     return pl.pallas_call(
         exchange_kernel,
@@ -274,9 +288,14 @@
             jax.ShapeDtypeStruct((DEV, TILE, TILE), jnp.bfloat16),
             jax.ShapeDtypeStruct((DEV,), jnp.int32),
         ),
-        in_specs=[smem, smem, vmem, any_space, any_space],
-        out_specs=(vmem, any_space, smem),
+        in_specs=[any_space] * 5,
+        out_specs=(any_space,) * 3,
         scratch_shapes=[
+            pltpu.SMEM((ACT, DEV), jnp.int32),
+            pltpu.SMEM((1,), jnp.int32),
+            pltpu.VMEM((1, PTS), jnp.float32),
+            pltpu.VMEM((1, PTS), jnp.float32),
+            pltpu.SMEM((DEV,), jnp.int32),
             chunk(jnp.float32),
             chunk(jnp.bfloat16),
             chunk(jnp.bfloat16),
@@ -295,6 +314,7 @@
             pltpu.SemaphoreType.DMA,
             pltpu.SemaphoreType.DMA,
             pltpu.SemaphoreType.REGULAR,
+            pltpu.SemaphoreType.DMA((5,)),
         ],
         compiler_params=pltpu.CompilerParams(
             collective_id=0, has_side_effects=True, vmem_limit_bytes=56 * 2**20
@@ -302,7 +322,12 @@
     )(act, cnt, kern, p, basis)
 
 
-def scatter_kernel(table, dens, came, out, dens_out, c_buf, o_buf, which, where, in_sem, out_sem):
+def scatter_kernel(
+    table_hbm, dens, came, out, dens_out, table, c_buf, o_buf, which, where, in_sem, out_sem, table_sem, dens_sem
+):
+    table_copy = pltpu.make_async_copy(table_hbm, table, table_sem)
+    dens_copy = pltpu.make_async_copy(dens, dens_out, dens_sem)
+    table_copy.start()
     def take(g):
         return pltpu.make_async_copy(came.at[:, pl.ds(g * CROWS, CROWS), :], c_buf.at[g], in_sem.at[g])
 
@@ -313,7 +338,15 @@
 
     for g in range(PARTS):
         take(g).start()
-    dens_out[...] = dens[...]
+    dens_copy.start()
+
+    def clear(n, carry):
+        for g in range(PARTS):
+            o_buf[g, pl.ds(n * 4, 4)] = jnp.zeros((4, CROWS, TILE), jnp.float32)
+        return carry
+
+    lax.fori_loop(0, PLACES // 4, clear, 0)
+    table_copy.wait()
 
     def compact(n, count):
         place = table[n]
@@ -328,12 +361,6 @@
     rounds = (count + UNROLL - 1) // UNROLL
 
     for g in range(PARTS):
-
-        def clear(n, carry, g=g):
-            o_buf[g, pl.ds(n * 8, 8)] = jnp.zeros((8, CROWS, TILE), jnp.float32)
-            return carry
-
-        lax.fori_loop(0, PLACES // 8, clear, 0)
         take(g).wait()
 
         def add(m, carry, g=g):
@@ -345,27 +372,29 @@
         put(g).start()
     for g in range(PARTS):
         put(g).wait()
+    dens_copy.wait()
 
 
 def scatter(table, dens, came):
     any_space = pl.BlockSpec(memory_space=pl.ANY)
-    smem = pl.BlockSpec(memory_space=pltpu.SMEM)
-    vmem = pl.BlockSpec(memory_space=pltpu.VMEM)
     return pl.pallas_call(
         scatter_kernel,
         out_shape=(
             jax.ShapeDtypeStruct((PLACES, TILE, TILE), jnp.float32),
             jax.ShapeDtypeStruct((1, PTS), jnp.float32),
         ),
-        in_specs=[smem, vmem, any_space],
-        out_specs=(any_space, vmem),
+        in_specs=[any_space] * 3,
+        out_specs=(any_space,) * 2,
         scratch_shapes=[
+            pltpu.SMEM((DEV,), jnp.int32),
             pltpu.VMEM((PARTS, DEV, CROWS, TILE), jnp.bfloat16),
             pltpu.VMEM((PARTS, PLACES + 1, CROWS, TILE), jnp.float32),
             pltpu.SMEM((DEV + UNROLL,), jnp.int32),
             pltpu.SMEM((DEV + UNROLL,), jnp.int32),
             pltpu.SemaphoreType.DMA((PARTS,)),
             pltpu.SemaphoreType.DMA((PARTS,)),
+            pltpu.SemaphoreType.DMA,
+            pltpu.SemaphoreType.DMA,
         ],
         compiler_params=pltpu.CompilerParams(vmem_limit_bytes=60 * 2**20),
     )(table, dens, came)

time: 122 us -> 119 us (0.975)
  Pallas kernels: 121 us -> 117 us
    pallas_call x1, Pallas kernels: 114 us -> 112 us  [exchange(): pl.pallas_call(exchange_kernel, out_shape=(jax.ShapeDtypeStruct((1, PTS),...]
where the time goes in v3:
time: 119 us
  Pallas kernels  117 us (98%)
  between operations  1.28 us (1%)
    pallas_call x1, Pallas kernels, exchange(): pl.pallas_call(exchange_kernel, out_shape=(jax.ShapeDtypeStruct((1, PTS),...  112 us
    pallas_call x1, Pallas kernels, scatter(): pl.pallas_call(scatter_kernel, out_shape=(jax.ShapeDtypeStruct((PLACES, T...  5.75 us

profile of v3, /device:TPU:1, one launch (start us, length us, event | category | flops | bytes accessed | tf_op | source)
XLA Modules:
  0.0 118.6 jit_solution(8710426243743881987)
XLA Ops:
  1.3 111.6 %shard_map.68 = (f32[1,4096]{1,0:T(1,128)}, bf16[128,128,128]{2,1,0:T(8,128)(2,1)}, s32[128]{0:T(128)}) custom-call(s32[8,128]{1,0:T(8,128)} %bitcast.8, s32[1]{0:T(128)S(6)} %copy.8.cnt_hbm, f32[1,4096]{1,0:T(1,128)} %kern_hbm.1, f32[128,128,128]{2,1,0:T(8,128)} %bitcast.6, bf16[4096,1024]{1,0:T(8,128)(2,1)} %bitcast.7), custom_call_target="tpu_custom_call" | custom-call | tf_op jit(solution)/shard_map/pallas_call | solution.py:284
  112.9 5.7 %shard_map.69 = (f32[128,128,128]{2,1,0:T(8,128)}, f32[1,4096]{1,0:T(1,128)}) custom-call(s32[128]{0:T(128)} %get-tuple-element.7.table_hbm, f32[1,4096]{1,0:T(1,128)} %get-tuple-element.8.dens, bf16[128,128,128]{2,1,0:T(8,128)(2,1)} %get-tuple-element.9.came), custom_call_target="tpu_custom_call" | custom-call | tf_op jit(solution)/shard_map/pallas_call | solution.py:380

commit v4 on v3

--- a/solution.py
+++ b/solution.py
@@ -19,8 +19,9 @@
 SIZES = (48, 32, 32, 16)
 FIRST = (0, 48, 80, 112)
 CHUNKS = len(SIZES)
-CROWS = 32
-PARTS = TILE // CROWS
+SUM_SIZES = (16, 48, 48, 16)
+SUM_FIRST = (0, 16, 64, 112)
+PARTS = len(SUM_SIZES)
 MIX = 23
 EARLY = 1
 UNUSED = 8
@@ -151,9 +152,9 @@
 
         @pl.when(c != UNUSED)
         def _(q=q):
+            send_to_others(q)
             if q >= EARLY:
                 send_to_peers(q)
-            send_to_others(q)
             pack(q, me)
             r_buf[q][me] = s_buf[q][me]
 
@@ -219,7 +220,7 @@
         lax.fori_loop(0, PTS // PT, weigh, 0)
 
         def part(turn_of, carry):
-            m = (turn_of + r // 2 + 2 * (r % 2) + c + c // 4) % 4
+            m = (3 * turn_of + r // 2 + 2 * (r % 2) + c + c // 4) % 4
             two = [basis[(2 * m + ii - start) & 7] for ii in range(2)]
             x = jnp.dot(weighted[...], jnp.concatenate(two, axis=1), preferred_element_type=jnp.float32)
             for ii in range(2):
@@ -329,11 +330,11 @@
     dens_copy = pltpu.make_async_copy(dens, dens_out, dens_sem)
     table_copy.start()
     def take(g):
-        return pltpu.make_async_copy(came.at[:, pl.ds(g * CROWS, CROWS), :], c_buf.at[g], in_sem.at[g])
+        return pltpu.make_async_copy(came.at[:, pl.ds(SUM_FIRST[g], SUM_SIZES[g]), :], c_buf[g], in_sem.at[g])
 
     def put(g):
         return pltpu.make_async_copy(
-            o_buf.at[g, pl.ds(0, PLACES)], out.at[:, pl.ds(g * CROWS, CROWS), :], out_sem.at[g]
+            o_buf[g].at[pl.ds(0, PLACES)], out.at[:, pl.ds(SUM_FIRST[g], SUM_SIZES[g]), :], out_sem.at[g]
         )
 
     for g in range(PARTS):
@@ -342,7 +343,7 @@
 
     def clear(n, carry):
         for g in range(PARTS):
-            o_buf[g, pl.ds(n * 4, 4)] = jnp.zeros((4, CROWS, TILE), jnp.float32)
+            o_buf[g][pl.ds(n * 4, 4)] = jnp.zeros((4, SUM_SIZES[g], TILE), jnp.float32)
         return carry
 
     lax.fori_loop(0, PLACES // 4, clear, 0)
@@ -365,7 +366,7 @@
 
         def add(m, carry, g=g):
             for e in range(UNROLL):
-                o_buf[g, where[m * UNROLL + e]] += c_buf[g, which[m * UNROLL + e]].astype(jnp.float32)
+                o_buf[g][where[m * UNROLL + e]] += c_buf[g][which[m * UNROLL + e]].astype(jnp.float32)
             return carry
 
         lax.fori_loop(0, rounds, add, 0)
@@ -387,8 +388,8 @@
         out_specs=(any_space,) * 2,
         scratch_shapes=[
             pltpu.SMEM((DEV,), jnp.int32),
-            pltpu.VMEM((PARTS, DEV, CROWS, TILE), jnp.bfloat16),
-            pltpu.VMEM((PARTS, PLACES + 1, CROWS, TILE), jnp.float32),
+            [pltpu.VMEM((DEV, rows, TILE), jnp.bfloat16) for rows in SUM_SIZES],
+            [pltpu.VMEM((PLACES + 1, rows, TILE), jnp.float32) for rows in SUM_SIZES],
             pltpu.SMEM((DEV + UNROLL,), jnp.int32),
             pltpu.SMEM((DEV + UNROLL,), jnp.int32),
             pltpu.SemaphoreType.DMA((PARTS,)),

time: 119 us -> 118 us (level)
  no operation moved by 1% of the time
where the time goes in v4:
time: 118 us
  Pallas kernels  117 us (99%)
  between operations  1.28 us (1%)
    pallas_call x1, Pallas kernels, exchange(): pl.pallas_call(exchange_kernel, out_shape=(jax.ShapeDtypeStruct((1, PTS),...  111 us
    pallas_call x1, Pallas kernels, scatter(): pl.pallas_call(scatter_kernel, out_shape=(jax.ShapeDtypeStruct((PLACES, T...  5.9 us

profile of v4, /device:TPU:1, one launch (start us, length us, event | category | flops | bytes accessed | tf_op | source)
XLA Modules:
  0.0 118.0 jit_solution(1473497202834611263)
XLA Ops:
  1.3 110.8 %shard_map.68 = (f32[1,4096]{1,0:T(1,128)}, bf16[128,128,128]{2,1,0:T(8,128)(2,1)}, s32[128]{0:T(128)}) custom-call(s32[8,128]{1,0:T(8,128)} %bitcast.8, s32[1]{0:T(128)S(6)} %copy.8.cnt_hbm, f32[1,4096]{1,0:T(1,128)} %kern_hbm.1, f32[128,128,128]{2,1,0:T(8,128)} %bitcast.6, bf16[4096,1024]{1,0:T(8,128)(2,1)} %bitcast.7), custom_call_target="tpu_custom_call" | custom-call | tf_op jit(solution)/shard_map/pallas_call | solution.py:285
  112.1 5.9 %shard_map.69 = (f32[128,128,128]{2,1,0:T(8,128)}, f32[1,4096]{1,0:T(1,128)}) custom-call(s32[128]{0:T(128)} %get-tuple-element.7.table_hbm, f32[1,4096]{1,0:T(1,128)} %get-tuple-element.8.dens, bf16[128,128,128]{2,1,0:T(8,128)(2,1)} %get-tuple-element.9.came), custom_call_target="tpu_custom_call" | custom-call | tf_op jit(solution)/shard_map/pallas_call | solution.py:381

commit v5 on v4

--- a/solution.py
+++ b/solution.py
@@ -25,8 +25,8 @@
 MIX = 23
 EARLY = 1
 UNUSED = 8
-PT = 512
-DPT = 1024
+PT = 1024
+DPT = 2048
 UNROLL = 4
 
 
@@ -226,7 +226,7 @@
             for ii in range(2):
                 for jj in range(2):
                     tile = x[jj * TILE : (jj + 1) * TILE, ii * TILE : (ii + 1) * TILE]
-                    h_send[2 * m + ii, 2 * pair + jj] = tile.T.astype(jnp.bfloat16)
+                    h_send[2 * m + ii, 2 * pair + jj] = tile.astype(jnp.bfloat16).T
             for ii in range(2):
                 give(2 * m + ii)
             return carry

time: 118 us -> 118 us (level)
  no operation moved by 1% of the time
where the time goes in v5:
time: 118 us
  Pallas kernels  116 us (98%)
  between operations  1.28 us (1%)
    pallas_call x1, Pallas kernels, exchange(): pl.pallas_call(exchange_kernel, out_shape=(jax.ShapeDtypeStruct((1, PTS),...  110 us
    pallas_call x1, Pallas kernels, scatter(): pl.pallas_call(scatter_kernel, out_shape=(jax.ShapeDtypeStruct((PLACES, T...  5.9 us

profile of v5, /device:TPU:1, one launch (start us, length us, event | category | flops | bytes accessed | tf_op | source)
XLA Modules:
  0.0 117.6 jit_solution(11997938024376276997)
XLA Ops:
  1.3 110.4 %shard_map.68 = (f32[1,4096]{1,0:T(1,128)}, bf16[128,128,128]{2,1,0:T(8,128)(2,1)}, s32[128]{0:T(128)}) custom-call(s32[8,128]{1,0:T(8,128)} %bitcast.8, s32[1]{0:T(128)S(6)} %copy.8.cnt_hbm, f32[1,4096]{1,0:T(1,128)} %kern_hbm.1, f32[128,128,128]{2,1,0:T(8,128)} %bitcast.6, bf16[4096,1024]{1,0:T(8,128)(2,1)} %bitcast.7), custom_call_target="tpu_custom_call" | custom-call | tf_op jit(solution)/shard_map/pallas_call | solution.py:285
  111.7 5.9 %shard_map.69 = (f32[128,128,128]{2,1,0:T(8,128)}, f32[1,4096]{1,0:T(1,128)}) custom-call(s32[128]{0:T(128)} %get-tuple-element.7.table_hbm, f32[1,4096]{1,0:T(1,128)} %get-tuple-element.8.dens, bf16[128,128,128]{2,1,0:T(8,128)(2,1)} %get-tuple-element.9.came), custom_call_target="tpu_custom_call" | custom-call | tf_op jit(solution)/shard_map/pallas_call | solution.py:381
